TPU v7x, 256 devices: a whole 4x4x8 slice. The times are simulated.
256 devices in a mesh: wide: 64 (over x, z_lo, y, core), narrow: 4 (over z_hi).
Axes of the slice: x: 4, y: 4, z: 8 (z_hi: 4, z_lo: 2; z = z_hi * 2 + z_lo), core: 2. Of those that a mesh axis runs over, the one named last changes fastest.
Arguments:
- source_features: bfloat16 [64, 128, 1024], P('wide'), may hold values from -6 to 6
- target_features: bfloat16 [32, 128, 1024], P('narrow', 'wide'), may hold values from -6 to 6
- target_in_taps: float32 [16, 9], replicated, may hold values from -2 to 2
- target_in_bias: float32 [16], replicated, may hold values from -3 to 3
- target_out_taps: float32 [16, 9], replicated, may hold values from -1 to 1
- source_in_taps: float32 [16, 9], replicated, may hold values from -2 to 2
- source_in_bias: float32 [16], replicated, may hold values from -3 to 3
- source_out_taps: float32 [16, 9], replicated, may hold values from -1 to 1
Outputs:
- consensus: bfloat16 [32, 128, 64, 128], P('narrow', 'wide')
All inputs are finite; a program needn't handle non-finite values.
Results may differ from a plain program's by a relative error of at most 0.0072.
Values may be sent and summed in bfloat16 or wider, within the bound.
A program may use at most 192 MiB of HBM per device.

v0:
```python
import jax
import jax.numpy as jnp
from jax import lax
from jax.sharding import PartitionSpec as P


def padded_2(block, sides, width):
    for axis, dim in sides:
        count = lax.axis_size(axis)
        forward = [(i, i + 1) for i in range(count - 1)]
        backward = [(target, source) for source, target in forward]
        low = lax.ppermute(
            lax.slice_in_dim(block, block.shape[dim] - width, None, axis=dim), axis, forward
        )
        high = lax.ppermute(lax.slice_in_dim(block, 0, width, axis=dim), axis, backward)
        block = jnp.concatenate([low, block, high], axis=dim)
    return block


def conv_valid(field, weights, first_axis, second_axis):
    size_one = field.shape[first_axis] - 2
    size_two = field.shape[second_axis] - 2
    total = None
    for a in range(3):
        rows = lax.slice_in_dim(field, a, a + size_one, axis=first_axis)
        for b in range(3):
            term = weights[3 * a + b] * lax.slice_in_dim(rows, b, b + size_two, axis=second_axis)
            total = term if total is None else total + term
    return total


def pad_axis(field, axis):
    widths = [(0, 0)] * field.ndim
    widths[axis] = (1, 1)
    return jnp.pad(field, widths)


def consensus_section(field, in_taps, in_bias, out_taps, first_axis, second_axis):
    padded = pad_axis(pad_axis(field.astype(jnp.float32), first_axis), second_axis)
    total = None
    for h in range(in_taps.shape[0]):
        hidden = jnp.maximum(
            conv_valid(padded, in_taps[h], first_axis, second_axis) + in_bias[h], 0.0
        )
        hidden = pad_axis(pad_axis(hidden, first_axis), second_axis)
        term = conv_valid(hidden, out_taps[h], first_axis, second_axis)
        total = term if total is None else total + term
    return jnp.maximum(total, 0.0)


def on_device(
    source_features,
    target_features,
    target_in_taps,
    target_in_bias,
    target_out_taps,
    source_in_taps,
    source_in_bias,
    source_out_taps,
):
    src_rows, src_cols, channels = source_features.shape
    tgt_rows = target_features.shape[0]
    scale = channels ** (-0.5)
    flat_source = source_features.reshape(src_rows * src_cols, channels)
    piece = lax.all_gather(target_features, "wide", axis=1, tiled=True)
    count = piece.shape[1]
    product = (
        jnp.dot(
            piece.reshape(tgt_rows * count, channels),
            flat_source.T,
            preferred_element_type=jnp.float32,
        )
        * scale
    )
    correlation = product.astype(jnp.bfloat16).reshape(tgt_rows, count, src_rows, src_cols)
    hidden_count = target_in_taps.shape[0]
    extended = padded_2(correlation, (("narrow", 0),), 2)
    padded = pad_axis(extended.astype(jnp.float32), 1)
    rows_here = tgt_rows + 2
    row_start = lax.axis_index("narrow") * tgt_rows
    global_rows = row_start - 1 + jnp.arange(rows_here, dtype=jnp.int32)
    all_rows = tgt_rows * lax.axis_size("narrow")
    inside = (
        ((global_rows >= 0) & (global_rows < all_rows))
        .astype(jnp.float32)
        .reshape(rows_here, 1, 1, 1)
    )
    total = None
    for h in range(hidden_count):
        hidden = (
            jnp.maximum(conv_valid(padded, target_in_taps[h], 0, 1) + target_in_bias[h], 0.0)
            * inside
        )
        term = conv_valid(pad_axis(hidden, 1), target_out_taps[h], 0, 1)
        total = term if total is None else total + term
    target_section = jnp.maximum(total, 0.0).astype(jnp.bfloat16)
    sectioned = consensus_section(
        lax.all_to_all(target_section, "wide", split_axis=1, concat_axis=2, tiled=True),
        source_in_taps,
        source_in_bias,
        source_out_taps,
        2,
        3,
    )
    return sectioned.astype(jnp.bfloat16)


def solution(mesh):
    placed = (P("wide", None, None), P("narrow", "wide", None), P(), P(), P(), P(), P(), P())
    return jax.shard_map(
        on_device,
        mesh=mesh,
        in_specs=placed,
        out_specs=P("narrow", "wide", None, None),
        check_vma=False,
    )
```

profile of v0, /device:TPU:1, one launch (start us, length us, event | category | flops | bytes accessed | tf_op | source)
XLA Modules:
  0.0 642.1 jit_solution(14112754118471764952)
XLA Ops:
  69.0 50.2 %all-gather.2.cloned.1.call-done = bf16[8,128,1024]{2,0,1:T(8,128)(2,1)} async-done(((bf16[8,2,1024]{2,0,1:T(8,128)(2,1)}), bf16[8,128,1024]{2,0,1:T(8,128)(2,1)}) %all-gather.2.cloned.1.call-update) | async-done | bytes 2097168 | tf_op jit(solution)/shard_map/all_gather | solution.py:65
  131.0 7.3 %maximum_multiply_fusion.15 = f32[10,128,1,128]{3,0,2,1:T(8,128)S(1)} fusion(f32[10]{0:T(128)S(1)} %and_convert_fusion, f32[]{:T(128)} %bitcast.17, f32[]{:T(128)} %bitcast.16, f32[]{:T(128)} %bitcast.15, f32[]{:T(128)} %bitcast.14, f32[]{:T(128)} %bitcast.13, f32[]{:T(128)} %bitcast.12, f32[]{:T(128)} %bitcast.11, f32[]{:T(128)} %bitcast.10, f32[]{:T(128)} %bitcast.9, ...), kind=kLoop, calls=%fused_computation.119 | loop fusion | flops 3276800 | bytes 4850216 | tf_op jit(solution)/shard_map/mul | solution.py:91
  141.3 7.4 %maximum_multiply_fusion = f32[10,128,1,128]{3,0,2,1:T(8,128)S(1)} fusion(f32[]{:T(128)} %bitcast.302, f32[]{:T(128)} %bitcast.301, f32[]{:T(128)} %bitcast.300, f32[]{:T(128)} %bitcast.299, f32[]{:T(128)} %bitcast.298, f32[]{:T(128)} %bitcast.297, f32[]{:T(128)} %bitcast.296, f32[]{:T(128)} %bitcast.295, f32[]{:T(128)} %bitcast.294, f32[]{:T(128)} %bitcast.293, ...), kind=kLoop, calls=%fused_computation.104 | loop fusion | flops 3276800 | bytes 4850216 | tf_op jit(solution)/shard_map/mul | solution.py:91
  148.6 7.3 %maximum_multiply_fusion.1 = f32[10,128,1,128]{3,0,2,1:T(8,128)S(1)} fusion(f32[]{:T(128)} %bitcast.283, f32[]{:T(128)} %bitcast.282, f32[]{:T(128)} %bitcast.281, f32[]{:T(128)} %bitcast.280, f32[]{:T(128)} %bitcast.279, f32[]{:T(128)} %bitcast.278, f32[]{:T(128)} %bitcast.277, f32[]{:T(128)} %bitcast.276, f32[]{:T(128)} %bitcast.275, f32[]{:T(128)} %bitcast.274, ...), kind=kLoop, calls=%fused_computation.105 | loop fusion | flops 3276800 | bytes 4850216 | tf_op jit(solution)/shard_map/mul | solution.py:91
  163.1 8.2 %maximum_multiply_fusion.3 = f32[10,128,1,128]{3,0,2,1:T(8,128)} fusion(f32[]{:T(128)} %bitcast.245, f32[]{:T(128)} %bitcast.244, f32[]{:T(128)} %bitcast.243, f32[]{:T(128)} %bitcast.242, f32[]{:T(128)} %bitcast.241, f32[]{:T(128)} %bitcast.240, f32[]{:T(128)} %bitcast.239, f32[]{:T(128)} %bitcast.238, f32[]{:T(128)} %bitcast.237, f32[]{:T(128)} %bitcast.236, ...), kind=kLoop, calls=%fused_computation.107 | loop fusion | flops 3276800 | bytes 4850216 | tf_op jit(solution)/shard_map/mul | solution.py:91
  171.3 8.1 %maximum_multiply_fusion.4 = f32[10,128,1,128]{3,0,2,1:T(8,128)} fusion(f32[]{:T(128)} %bitcast.226, f32[]{:T(128)} %bitcast.225, f32[]{:T(128)} %bitcast.224, f32[]{:T(128)} %bitcast.223, f32[]{:T(128)} %bitcast.222, f32[]{:T(128)} %bitcast.221, f32[]{:T(128)} %bitcast.220, f32[]{:T(128)} %bitcast.219, f32[]{:T(128)} %bitcast.218, f32[]{:T(128)} %bitcast.217, ...), kind=kLoop, calls=%fused_computation.108 | loop fusion | flops 3276800 | bytes 4850216 | tf_op jit(solution)/shard_map/mul | solution.py:91
  179.4 8.1 %maximum_multiply_fusion.5 = f32[10,128,1,128]{3,0,2,1:T(8,128)} fusion(f32[]{:T(128)} %bitcast.207, f32[]{:T(128)} %bitcast.206, f32[]{:T(128)} %bitcast.205, f32[]{:T(128)} %bitcast.204, f32[]{:T(128)} %bitcast.203, f32[]{:T(128)} %bitcast.202, f32[]{:T(128)} %bitcast.201, f32[]{:T(128)} %bitcast.200, f32[]{:T(128)} %bitcast.199, f32[]{:T(128)} %bitcast.198, ...), kind=kLoop, calls=%fused_computation.109 | loop fusion | flops 3276800 | bytes 4850216 | tf_op jit(solution)/shard_map/mul | solution.py:91
  187.6 8.0 %maximum_multiply_fusion.6 = f32[10,128,1,128]{3,0,2,1:T(8,128)} fusion(f32[]{:T(128)} %bitcast.188, f32[]{:T(128)} %bitcast.187, f32[]{:T(128)} %bitcast.186, f32[]{:T(128)} %bitcast.185, f32[]{:T(128)} %bitcast.184, f32[]{:T(128)} %bitcast.183, f32[]{:T(128)} %bitcast.182, f32[]{:T(128)} %bitcast.181, f32[]{:T(128)} %bitcast.180, f32[]{:T(128)} %bitcast.179, ...), kind=kLoop, calls=%fused_computation.110 | loop fusion | flops 3276800 | bytes 4850216 | tf_op jit(solution)/shard_map/mul | solution.py:91
  195.6 7.9 %maximum_multiply_fusion.7 = f32[10,128,1,128]{3,0,2,1:T(8,128)} fusion(f32[]{:T(128)} %bitcast.169, f32[]{:T(128)} %bitcast.168, f32[]{:T(128)} %bitcast.167, f32[]{:T(128)} %bitcast.166, f32[]{:T(128)} %bitcast.165, f32[]{:T(128)} %bitcast.164, f32[]{:T(128)} %bitcast.163, f32[]{:T(128)} %bitcast.162, f32[]{:T(128)} %bitcast.161, f32[]{:T(128)} %bitcast.160, ...), kind=kLoop, calls=%fused_computation.111 | loop fusion | flops 3276800 | bytes 4850216 | tf_op jit(solution)/shard_map/mul | solution.py:91
  203.4 8.2 %maximum_multiply_fusion.8 = f32[10,128,1,128]{3,0,2,1:T(8,128)} fusion(f32[]{:T(128)} %bitcast.150, f32[]{:T(128)} %bitcast.149, f32[]{:T(128)} %bitcast.148, f32[]{:T(128)} %bitcast.147, f32[]{:T(128)} %bitcast.146, f32[]{:T(128)} %bitcast.145, f32[]{:T(128)} %bitcast.144, f32[]{:T(128)} %bitcast.143, f32[]{:T(128)} %bitcast.142, f32[]{:T(128)} %bitcast.141, ...), kind=kLoop, calls=%fused_computation.112 | loop fusion | flops 3276800 | bytes 4850216 | tf_op jit(solution)/shard_map/mul | solution.py:91
  211.6 8.3 %maximum_multiply_fusion.9 = f32[10,128,1,128]{3,0,2,1:T(8,128)} fusion(f32[]{:T(128)} %bitcast.131, f32[]{:T(128)} %bitcast.130, f32[]{:T(128)} %bitcast.129, f32[]{:T(128)} %bitcast.128, f32[]{:T(128)} %bitcast.127, f32[]{:T(128)} %bitcast.126, f32[]{:T(128)} %bitcast.125, f32[]{:T(128)} %bitcast.124, f32[]{:T(128)} %bitcast.123, f32[]{:T(128)} %bitcast.122, ...), kind=kLoop, calls=%fused_computation.113 | loop fusion | flops 3276800 | bytes 4850216 | tf_op jit(solution)/shard_map/mul | solution.py:91
  220.0 8.2 %maximum_multiply_fusion.10 = f32[10,128,1,128]{3,0,2,1:T(8,128)} fusion(f32[]{:T(128)} %bitcast.112, f32[]{:T(128)} %bitcast.111, f32[]{:T(128)} %bitcast.110, f32[]{:T(128)} %bitcast.109, f32[]{:T(128)} %bitcast.108, f32[]{:T(128)} %bitcast.107, f32[]{:T(128)} %bitcast.106, f32[]{:T(128)} %bitcast.105, f32[]{:T(128)} %bitcast.104, f32[]{:T(128)} %bitcast.103, ...), kind=kLoop, calls=%fused_computation.114 | loop fusion | flops 3276800 | bytes 4850216 | tf_op jit(solution)/shard_map/mul | solution.py:91
  228.2 8.4 %maximum_multiply_fusion.11 = f32[10,128,1,128]{3,0,2,1:T(8,128)} fusion(f32[]{:T(128)} %bitcast.93, f32[]{:T(128)} %bitcast.92, f32[]{:T(128)} %bitcast.91, f32[]{:T(128)} %bitcast.90, f32[]{:T(128)} %bitcast.89, f32[]{:T(128)} %bitcast.88, f32[]{:T(128)} %bitcast.87, f32[]{:T(128)} %bitcast.86, f32[]{:T(128)} %bitcast.85, f32[]{:T(128)} %bitcast.84, ...), kind=kLoop, calls=%fused_computation.115 | loop fusion | flops 3276800 | bytes 4850216 | tf_op jit(solution)/shard_map/mul | solution.py:91
  236.5 8.1 %maximum_multiply_fusion.12 = f32[10,128,1,128]{3,0,2,1:T(8,128)} fusion(f32[]{:T(128)} %bitcast.74, f32[]{:T(128)} %bitcast.73, f32[]{:T(128)} %bitcast.72, f32[]{:T(128)} %bitcast.71, f32[]{:T(128)} %bitcast.70, f32[]{:T(128)} %bitcast.69, f32[]{:T(128)} %bitcast.68, f32[]{:T(128)} %bitcast.67, f32[]{:T(128)} %bitcast.66, f32[]{:T(128)} %bitcast.65, ...), kind=kLoop, calls=%fused_computation.116 | loop fusion | flops 3276800 | bytes 4850216 | tf_op jit(solution)/shard_map/mul | solution.py:91
  244.6 8.4 %maximum_multiply_fusion.13 = f32[10,128,1,128]{3,0,2,1:T(8,128)} fusion(f32[]{:T(128)} %bitcast.55, f32[]{:T(128)} %bitcast.54, f32[]{:T(128)} %bitcast.53, f32[]{:T(128)} %bitcast.52, f32[]{:T(128)} %bitcast.51, f32[]{:T(128)} %bitcast.50, f32[]{:T(128)} %bitcast.49, f32[]{:T(128)} %bitcast.48, f32[]{:T(128)} %bitcast.47, f32[]{:T(128)} %bitcast.46, ...), kind=kLoop, calls=%fused_computation.117 | loop fusion | flops 3276800 | bytes 4850216 | tf_op jit(solution)/shard_map/mul | solution.py:91
  253.0 8.4 %maximum_multiply_fusion.14 = f32[10,128,1,128]{3,0,2,1:T(8,128)} fusion(f32[]{:T(128)} %bitcast.36, f32[]{:T(128)} %bitcast.35, f32[]{:T(128)} %bitcast.34, f32[]{:T(128)} %bitcast.33, f32[]{:T(128)} %bitcast.32, f32[]{:T(128)} %bitcast.31, f32[]{:T(128)} %bitcast.30, f32[]{:T(128)} %bitcast.29, f32[]{:T(128)} %bitcast.28, f32[]{:T(128)} %bitcast.27, ...), kind=kLoop, calls=%fused_computation.118 | loop fusion | flops 3276800 | bytes 4850216 | tf_op jit(solution)/shard_map/mul | solution.py:91
  261.4 133.5 %fusion.610 = bf16[8,128,1,128]{3,0,2,1:T(8,128)(2,1)} fusion(f32[10,128,1,128]{3,0,2,1:T(8,128)S(1)} %maximum_multiply_fusion, f32[]{:T(128)} %bitcast.310, f32[]{:T(128)} %bitcast.309, f32[]{:T(128)} %bitcast.308, f32[]{:T(128)} %bitcast.307, f32[]{:T(128)} %bitcast.306, f32[]{:T(128)} %bitcast.305, f32[]{:T(128)} %bitcast.304, f32[]{:T(128)} %bitcast.303, ...), kind=kLoop, calls=%fused_computation.882 | loop fusion | flops 37486592 | bytes 42277376 | tf_op jit(solution)/shard_map/convert_element_type | solution.py:96
  395.0 8.0 %all-to-all-start = ((bf16[8,128,1,128]{3,0,2,1:T(8,128)(2,1)}), bf16[8,128,1,128]{3,0,2,1:T(8,128)(2,1)S(1)}, u32[]{:S(2)}, u32[]{:S(2)}) async-start(bf16[8,128,1,128]{3,0,2,1:T(8,128)(2,1)} %fusion.610), calls=%async_computation | async-start | bytes 524288 | tf_op jit(solution)/shard_map/all_to_all | solution.py:98
  448.3 7.2 %fusion.573 = f32[8,2,64,128]{3,0,1,2:T(8,128)S(1)} fusion(bf16[8,64,2,1,128]{4,0,2,1,3:T(8,128)(2,1)S(1)} %bitcast.887, f32[]{:T(128)} %bitcast.516, f32[]{:T(128)} %bitcast.515, f32[]{:T(128)} %bitcast.514, f32[]{:T(128)} %bitcast.513, f32[]{:T(128)} %bitcast.512, f32[]{:T(128)} %bitcast.511, f32[]{:T(128)} %bitcast.510, f32[]{:T(128)} %bitcast.509, ...), kind=kLoop, calls=%fused_computation.844 | loop fusion | flops 2621440 | bytes 1851432 | tf_op jit(solution)/shard_map/max | solution.py:42
  455.5 7.2 %fusion.566 = f32[8,2,64,128]{3,0,1,2:T(8,128)S(1)} fusion(bf16[8,64,2,1,128]{4,0,2,1,3:T(8,128)(2,1)S(1)} %bitcast.888, f32[]{:T(128)} %bitcast.497, f32[]{:T(128)} %bitcast.496, f32[]{:T(128)} %bitcast.495, f32[]{:T(128)} %bitcast.494, f32[]{:T(128)} %bitcast.493, f32[]{:T(128)} %bitcast.492, f32[]{:T(128)} %bitcast.491, f32[]{:T(128)} %bitcast.490, ...), kind=kLoop, calls=%fused_computation.837 | loop fusion | flops 2621440 | bytes 1851432 | tf_op jit(solution)/shard_map/max | solution.py:42
  498.4 7.2 %fusion.524 = f32[8,2,64,128]{3,0,1,2:T(8,128)S(1)} fusion(bf16[8,64,2,1,128]{4,0,2,1,3:T(8,128)(2,1)S(1)} %bitcast.894, f32[]{:T(128)} %bitcast.383, f32[]{:T(128)} %bitcast.382, f32[]{:T(128)} %bitcast.381, f32[]{:T(128)} %bitcast.380, f32[]{:T(128)} %bitcast.379, f32[]{:T(128)} %bitcast.378, f32[]{:T(128)} %bitcast.377, f32[]{:T(128)} %bitcast.376, ...), kind=kLoop, calls=%fused_computation.795 | loop fusion | flops 2621440 | bytes 1851432 | tf_op jit(solution)/shard_map/max | solution.py:42
  512.8 7.3 %fusion.510 = f32[8,2,64,128]{3,0,1,2:T(8,128)S(1)} fusion(bf16[8,64,2,1,128]{4,0,2,1,3:T(8,128)(2,1)S(1)} %bitcast.896, f32[]{:T(128)} %bitcast.345, f32[]{:T(128)} %bitcast.344, f32[]{:T(128)} %bitcast.343, f32[]{:T(128)} %bitcast.342, f32[]{:T(128)} %bitcast.341, f32[]{:T(128)} %bitcast.339, f32[]{:T(128)} %bitcast.338, f32[]{:T(128)} %bitcast.337, ...), kind=kLoop, calls=%fused_computation.781 | loop fusion | flops 2621440 | bytes 1851432 | tf_op jit(solution)/shard_map/max | solution.py:42
  520.2 7.7 %broadcast_multiply_fusion = (f32[8,2,64,128]{3,0,1,2:T(8,128)S(1)}, f32[8,2,64,128]{3,0,1,2:T(8,128)S(1)}) fusion(f32[]{:T(128)} %bitcast.329, f32[]{:T(128)} %bitcast.325, f32[]{:T(128)} %bitcast.324, f32[]{:T(128)} %bitcast.323, f32[]{:T(128)} %bitcast.322, f32[]{:T(128)} %bitcast.321, bf16[8,64,2,1,128]{4,0,2,1,3:T(8,128)(2,1)S(1)} %bitcast.897, ...), kind=kLoop, calls=%fused_computation.884 | loop fusion | flops 2752512 | bytes 2375724 | tf_op jit(solution)/shard_map/mul | solution.py:27
  527.9 106.1 %fusion.609 = bf16[8,2,64,128]{3,0,1,2:T(8,128)(2,1)S(1)} fusion(f32[8,2,66,128]{3,0,1,2:T(8,128)S(1)} %pad.206, f32[8,2,64,128]{3,0,1,2:T(8,128)S(1)} %fusion.608, f32[]{:T(128)} %bitcast.619, f32[]{:T(128)} %bitcast.618, f32[]{:T(128)} %bitcast.617, f32[]{:T(128)} %bitcast.616, f32[]{:T(128)} %bitcast.615, f32[]{:T(128)} %bitcast.614, f32[]{:T(128)} %bitcast.613, ...), kind=kLoop, calls=%fused_computation.881 | loop fusion | flops 37748736 | bytes 34079292 | tf_op jit(solution)/shard_map/convert_element_type | solution.py:105
  (90 shorter events, 173.0 us)
Async XLA Ops:
  6.5 115.4 %copy-start = (bf16[1,128,1024]{2,1,0:T(8,128)(2,1)S(1)}, bf16[1,128,1024]{2,1,0:T(8,128)(2,1)}, u32[]{:S(2)}) copy-start(bf16[1,128,1024]{2,1,0:T(8,128)(2,1)} %param.8) | copy-start | bytes 786436
  6.5 112.7 %all-gather.2.cloned.1.call-start = ((), (), s32[]{:S(2)}) async-start(), calls=%async_computation.1 | async-start | bytes 2129920 | tf_op jit(solution)/shard_map/all_gather | solution.py:65
  122.8 7.9 %collective-permute-start.1 = (bf16[2,128,1,128]{3,0,2,1:T(2,128)(2,1)S(1)}, bf16[2,128,1,128]{3,0,2,1:T(2,128)(2,1)S(1)}, u32[]{:S(2)}, u32[]{:S(2)}) collective-permute-start(bf16[2,128,1,128]{3,0,2,1:T(2,128)(2,1)S(1)} %copy.22), channel_id=1, source_target_pairs={{1,0},{2,1},{3,2},{5,4},{6,5},{7,6},{9,8},{10,9},{11,10},{13,12},{... | collective-permute-start | bytes 196616 | tf_op jit(solution)/shard_map/ppermute | solution.py:15
  124.1 6.5 %collective-permute-start = (bf16[2,128,1,128]{3,0,2,1:T(2,128)(2,1)S(1)}, bf16[2,128,1,128]{3,0,2,1:T(2,128)(2,1)S(1)}, u32[]{:S(2)}, u32[]{:S(2)}) collective-permute-start(bf16[2,128,1,128]{3,0,2,1:T(2,128)(2,1)S(1)} %copy.21), channel_id=1, source_target_pairs={{0,1},{1,2},{2,3},{4,5},{5,6},{6,7},{8,9},{9,10},{10,11},{12,13},{... | collective-permute-start | bytes 196616 | tf_op jit(solution)/shard_map/ppermute | solution.py:12
  138.2 3.0 copy-start.1
  261.4 141.6 %copy-start.2 = (f32[16,9]{1,0:T(8,128)S(1)}, f32[16,9]{1,0:T(8,128)}, u32[]{:S(2)}) copy-start(f32[16,9]{1,0:T(8,128)} %param.15) | copy-start | bytes 1732
  261.4 142.3 %copy-start.3 = (f32[16,9]{1,0:T(8,128)S(1)}, f32[16,9]{1,0:T(8,128)}, u32[]{:S(2)}) copy-start(f32[16,9]{1,0:T(8,128)} %param.13) | copy-start | bytes 1732
  395.0 17.6 %all-to-all-start = ((bf16[8,128,1,128]{3,0,2,1:T(8,128)(2,1)}), bf16[8,128,1,128]{3,0,2,1:T(8,128)(2,1)S(1)}, u32[]{:S(2)}, u32[]{:S(2)}) async-start(bf16[8,128,1,128]{3,0,2,1:T(8,128)(2,1)} %fusion.610), calls=%async_computation | async-start | bytes 524288 | tf_op jit(solution)/shard_map/all_to_all | solution.py:98
Sparse Core Ops, SparseCore 0:
  9.2 109.9 all-gather.1
where the time goes:
time: 654 us; the launch traced here: 642 us
  other arithmetic  485 us (74%)
  local copies, waits for them, and re-layouts  70.3 us (11%)
  waiting for transfers between devices  57.2 us (9%)
  starting transfers between devices  14.7 us (2%)
  between operations  14.4 us (2%)
    convert_element_type x1, other arithmetic, on_device(): target_section = jnp.maximum(total, 0.0).astype(jnp.bfloat16)  134 us
    mul x16, other arithmetic, on_device(): jnp.maximum(conv_valid(padded, target_in_taps[h], 0, 1) + target_in_bias[...  127 us
    max x15, other arithmetic, consensus_section(): jnp.maximum(conv_valid(padded, in_taps[h], first_axis, second_axis) + in_...  107 us
    convert_element_type x1, other arithmetic, on_device(): return sectioned.astype(jnp.bfloat16)  106 us
    slice x32, local copies, waits for them, and re-layouts, conv_valid(): weights[3 * a + b]  60.5 us
    all_gather x1, waiting for transfers between devices, on_device(): piece = lax.all_gather(target_features, 'wide', axis=1, tiled=True)  50.2 us
  transfers between devices with their start and end apart: 4, of which 3 were waited for; matrix products, arithmetic and copies ran while one was open for 10% of the time, Pallas kernels for 0%

commit v1 on v0

--- a/solution.py
+++ b/solution.py
@@ -62,7 +62,9 @@
     tgt_rows = target_features.shape[0]
     scale = channels ** (-0.5)
     flat_source = source_features.reshape(src_rows * src_cols, channels)
-    piece = lax.all_gather(target_features, "wide", axis=1, tiled=True)
+    piece = jnp.concatenate(
+        lax.all_to_all(jnp.stack([target_features] * lax.axis_size("wide")), "wide", 0, 0), axis=1
+    )
     count = piece.shape[1]
     product = (
         jnp.dot(

time: 654 us -> 573 us (0.88)
  waiting for transfers between devices: 57.2 us -> 15.6 us
  local copies, waits for them, and re-layouts: 70.3 us -> 36.2 us
  between operations: 14.4 us -> 0.75 us
  starting transfers between devices: 14.7 us -> 23.5 us
    all_gather x1 -> x0, waiting for transfers between devices: 50.2 us -> none  [on_device(): piece = lax.all_gather(target_features, 'wide', axis=1, tiled=True)]
    slice x32, local copies, waits for them, and re-layouts: 60.5 us -> 23.1 us  [conv_valid(): weights[3 * a + b]]
    all_to_all x0 -> x1, starting transfers between devices: none -> 10.5 us  [on_device(): lax.all_to_all(jnp.stack([target_features] * lax.axis_size('wide')), 'wid...]
    all_to_all x0 -> x1, waiting for transfers between devices: none -> 8.03 us  [on_device(): lax.all_to_all(jnp.stack([target_features] * lax.axis_size('wide')), 'wid...]
    another operation x0 -> x2, local copies, waits for them, and re-layouts: none -> 6.92 us  [the longest x1 4.17 us: on_device(): jnp.stack([target_features] * lax.axis_size('wide'))]
  transfers between devices with their start and end apart: 4 -> 4, of which waited for: 3 -> 3; matrix products, arithmetic and copies ran while one was open for 10% -> 4% of each run, Pallas kernels for 0% -> 0%
where the time goes in v1:
time: 573 us; the launch traced here: 562 us
  other arithmetic  485 us (85%)
  local copies, waits for them, and re-layouts  36.2 us (6%)
  starting transfers between devices  23.5 us (4%)
  waiting for transfers between devices  15.6 us (3%)
    convert_element_type x1, other arithmetic, on_device(): target_section = jnp.maximum(total, 0.0).astype(jnp.bfloat16)  133 us
    mul x16, other arithmetic, on_device(): jnp.maximum(conv_valid(padded, target_in_taps[h], 0, 1) + target_in_bias[...  128 us
    max x15, other arithmetic, consensus_section(): jnp.maximum(conv_valid(padded, in_taps[h], first_axis, second_axis) + in_...  107 us
    convert_element_type x1, other arithmetic, on_device(): return sectioned.astype(jnp.bfloat16)  106 us
    slice x32, local copies, waits for them, and re-layouts, conv_valid(): weights[3 * a + b]  23.1 us
  transfers between devices with their start and end apart: 4, of which 3 were waited for; matrix products, arithmetic and copies ran while one was open for 4% of the time, Pallas kernels for 0%

profile of v1, /device:TPU:1, one launch (start us, length us, event | category | flops | bytes accessed | tf_op | source)
XLA Modules:
  0.0 561.5 jit_solution(15564337623032634979)
XLA Ops:
  4.2 10.5 %all-to-all-start = ((bf16[64,8,2,1024]{3,2,1,0:T(2,128)(2,1)}), bf16[64,8,2,1024]{3,2,1,0:T(2,128)(2,1)S(1)}, u32[]{:S(2)}, u32[]{:S(2)}) async-start(bf16[64,8,2,1024]{3,2,1,0:T(2,128)(2,1)} %stack.2), calls=%async_computation | async-start | bytes 4194304 | tf_op jit(solution)/shard_map/all_to_all | solution.py:66
  35.7 8.0 %all-to-all-done = bf16[64,8,2,1024]{3,2,1,0:T(2,128)(2,1)S(1)} async-done(((bf16[64,8,2,1024]{3,2,1,0:T(2,128)(2,1)}), bf16[64,8,2,1024]{3,2,1,0:T(2,128)(2,1)S(1)}, u32[]{:S(2)}, u32[]{:S(2)}) %all-to-all-start) | async-done | bytes 2097184 | tf_op jit(solution)/shard_map/all_to_all | solution.py:66
  69.5 7.2 %maximum_multiply_fusion = f32[10,128,1,128]{3,0,2,1:T(8,128)S(1)} fusion(f32[]{:T(128)} %bitcast.302, f32[]{:T(128)} %bitcast.301, f32[]{:T(128)} %bitcast.300, f32[]{:T(128)} %bitcast.299, f32[]{:T(128)} %bitcast.298, f32[]{:T(128)} %bitcast.297, f32[]{:T(128)} %bitcast.296, f32[]{:T(128)} %bitcast.295, f32[]{:T(128)} %bitcast.294, f32[]{:T(128)} %bitcast.293, ...), kind=kLoop, calls=%fused_computation.104 | loop fusion | flops 3276800 | bytes 4850216 | tf_op jit(solution)/shard_map/mul | solution.py:93
  76.8 7.3 %maximum_multiply_fusion.1 = f32[10,128,1,128]{3,0,2,1:T(8,128)S(1)} fusion(f32[]{:T(128)} %bitcast.283, f32[]{:T(128)} %bitcast.282, f32[]{:T(128)} %bitcast.281, f32[]{:T(128)} %bitcast.280, f32[]{:T(128)} %bitcast.279, f32[]{:T(128)} %bitcast.278, f32[]{:T(128)} %bitcast.277, f32[]{:T(128)} %bitcast.276, f32[]{:T(128)} %bitcast.275, f32[]{:T(128)} %bitcast.274, ...), kind=kLoop, calls=%fused_computation.105 | loop fusion | flops 3276800 | bytes 4850216 | tf_op jit(solution)/shard_map/mul | solution.py:93
  84.1 7.2 %maximum_multiply_fusion.2 = f32[10,128,1,128]{3,0,2,1:T(8,128)S(1)} fusion(f32[]{:T(128)} %bitcast.264, f32[]{:T(128)} %bitcast.263, f32[]{:T(128)} %bitcast.262, f32[]{:T(128)} %bitcast.261, f32[]{:T(128)} %bitcast.260, f32[]{:T(128)} %bitcast.259, f32[]{:T(128)} %bitcast.258, f32[]{:T(128)} %bitcast.257, f32[]{:T(128)} %bitcast.256, f32[]{:T(128)} %bitcast.255, ...), kind=kLoop, calls=%fused_computation.106 | loop fusion | flops 3276800 | bytes 4850216 | tf_op jit(solution)/shard_map/mul | solution.py:93
  91.3 8.3 %maximum_multiply_fusion.3 = f32[10,128,1,128]{3,0,2,1:T(8,128)} fusion(f32[]{:T(128)} %bitcast.245, f32[]{:T(128)} %bitcast.244, f32[]{:T(128)} %bitcast.243, f32[]{:T(128)} %bitcast.242, f32[]{:T(128)} %bitcast.241, f32[]{:T(128)} %bitcast.240, f32[]{:T(128)} %bitcast.239, f32[]{:T(128)} %bitcast.238, f32[]{:T(128)} %bitcast.237, f32[]{:T(128)} %bitcast.236, ...), kind=kLoop, calls=%fused_computation.107 | loop fusion | flops 3276800 | bytes 4850216 | tf_op jit(solution)/shard_map/mul | solution.py:93
  99.6 8.1 %maximum_multiply_fusion.4 = f32[10,128,1,128]{3,0,2,1:T(8,128)} fusion(f32[]{:T(128)} %bitcast.226, f32[]{:T(128)} %bitcast.225, f32[]{:T(128)} %bitcast.224, f32[]{:T(128)} %bitcast.223, f32[]{:T(128)} %bitcast.222, f32[]{:T(128)} %bitcast.221, f32[]{:T(128)} %bitcast.220, f32[]{:T(128)} %bitcast.219, f32[]{:T(128)} %bitcast.218, f32[]{:T(128)} %bitcast.217, ...), kind=kLoop, calls=%fused_computation.108 | loop fusion | flops 3276800 | bytes 4850216 | tf_op jit(solution)/shard_map/mul | solution.py:93
  107.7 8.2 %maximum_multiply_fusion.5 = f32[10,128,1,128]{3,0,2,1:T(8,128)} fusion(f32[]{:T(128)} %bitcast.207, f32[]{:T(128)} %bitcast.206, f32[]{:T(128)} %bitcast.205, f32[]{:T(128)} %bitcast.204, f32[]{:T(128)} %bitcast.203, f32[]{:T(128)} %bitcast.202, f32[]{:T(128)} %bitcast.201, f32[]{:T(128)} %bitcast.200, f32[]{:T(128)} %bitcast.199, f32[]{:T(128)} %bitcast.198, ...), kind=kLoop, calls=%fused_computation.109 | loop fusion | flops 3276800 | bytes 4850216 | tf_op jit(solution)/shard_map/mul | solution.py:93
  115.9 8.2 %maximum_multiply_fusion.6 = f32[10,128,1,128]{3,0,2,1:T(8,128)} fusion(f32[]{:T(128)} %bitcast.188, f32[]{:T(128)} %bitcast.187, f32[]{:T(128)} %bitcast.186, f32[]{:T(128)} %bitcast.185, f32[]{:T(128)} %bitcast.184, f32[]{:T(128)} %bitcast.183, f32[]{:T(128)} %bitcast.182, f32[]{:T(128)} %bitcast.181, f32[]{:T(128)} %bitcast.180, f32[]{:T(128)} %bitcast.179, ...), kind=kLoop, calls=%fused_computation.110 | loop fusion | flops 3276800 | bytes 4850216 | tf_op jit(solution)/shard_map/mul | solution.py:93
  124.0 7.9 %maximum_multiply_fusion.7 = f32[10,128,1,128]{3,0,2,1:T(8,128)} fusion(f32[]{:T(128)} %bitcast.169, f32[]{:T(128)} %bitcast.168, f32[]{:T(128)} %bitcast.167, f32[]{:T(128)} %bitcast.166, f32[]{:T(128)} %bitcast.165, f32[]{:T(128)} %bitcast.164, f32[]{:T(128)} %bitcast.163, f32[]{:T(128)} %bitcast.162, f32[]{:T(128)} %bitcast.161, f32[]{:T(128)} %bitcast.160, ...), kind=kLoop, calls=%fused_computation.111 | loop fusion | flops 3276800 | bytes 4850216 | tf_op jit(solution)/shard_map/mul | solution.py:93
  131.9 8.1 %maximum_multiply_fusion.8 = f32[10,128,1,128]{3,0,2,1:T(8,128)} fusion(f32[]{:T(128)} %bitcast.150, f32[]{:T(128)} %bitcast.149, f32[]{:T(128)} %bitcast.148, f32[]{:T(128)} %bitcast.147, f32[]{:T(128)} %bitcast.146, f32[]{:T(128)} %bitcast.145, f32[]{:T(128)} %bitcast.144, f32[]{:T(128)} %bitcast.143, f32[]{:T(128)} %bitcast.142, f32[]{:T(128)} %bitcast.141, ...), kind=kLoop, calls=%fused_computation.112 | loop fusion | flops 3276800 | bytes 4850216 | tf_op jit(solution)/shard_map/mul | solution.py:93
  140.0 8.6 %maximum_multiply_fusion.9 = f32[10,128,1,128]{3,0,2,1:T(8,128)} fusion(f32[]{:T(128)} %bitcast.131, f32[]{:T(128)} %bitcast.130, f32[]{:T(128)} %bitcast.129, f32[]{:T(128)} %bitcast.128, f32[]{:T(128)} %bitcast.127, f32[]{:T(128)} %bitcast.126, f32[]{:T(128)} %bitcast.125, f32[]{:T(128)} %bitcast.124, f32[]{:T(128)} %bitcast.123, f32[]{:T(128)} %bitcast.122, ...), kind=kLoop, calls=%fused_computation.113 | loop fusion | flops 3276800 | bytes 4850216 | tf_op jit(solution)/shard_map/mul | solution.py:93
  148.6 8.1 %maximum_multiply_fusion.10 = f32[10,128,1,128]{3,0,2,1:T(8,128)} fusion(f32[]{:T(128)} %bitcast.112, f32[]{:T(128)} %bitcast.111, f32[]{:T(128)} %bitcast.110, f32[]{:T(128)} %bitcast.109, f32[]{:T(128)} %bitcast.108, f32[]{:T(128)} %bitcast.107, f32[]{:T(128)} %bitcast.106, f32[]{:T(128)} %bitcast.105, f32[]{:T(128)} %bitcast.104, f32[]{:T(128)} %bitcast.103, ...), kind=kLoop, calls=%fused_computation.114 | loop fusion | flops 3276800 | bytes 4850216 | tf_op jit(solution)/shard_map/mul | solution.py:93
  156.7 8.4 %maximum_multiply_fusion.11 = f32[10,128,1,128]{3,0,2,1:T(8,128)} fusion(f32[]{:T(128)} %bitcast.93, f32[]{:T(128)} %bitcast.92, f32[]{:T(128)} %bitcast.91, f32[]{:T(128)} %bitcast.90, f32[]{:T(128)} %bitcast.89, f32[]{:T(128)} %bitcast.88, f32[]{:T(128)} %bitcast.87, f32[]{:T(128)} %bitcast.86, f32[]{:T(128)} %bitcast.85, f32[]{:T(128)} %bitcast.84, ...), kind=kLoop, calls=%fused_computation.115 | loop fusion | flops 3276800 | bytes 4850216 | tf_op jit(solution)/shard_map/mul | solution.py:93
  165.1 8.5 %maximum_multiply_fusion.12 = f32[10,128,1,128]{3,0,2,1:T(8,128)} fusion(f32[]{:T(128)} %bitcast.74, f32[]{:T(128)} %bitcast.73, f32[]{:T(128)} %bitcast.72, f32[]{:T(128)} %bitcast.71, f32[]{:T(128)} %bitcast.70, f32[]{:T(128)} %bitcast.69, f32[]{:T(128)} %bitcast.68, f32[]{:T(128)} %bitcast.67, f32[]{:T(128)} %bitcast.66, f32[]{:T(128)} %bitcast.65, ...), kind=kLoop, calls=%fused_computation.116 | loop fusion | flops 3276800 | bytes 4850216 | tf_op jit(solution)/shard_map/mul | solution.py:93
  173.6 8.3 %maximum_multiply_fusion.13 = f32[10,128,1,128]{3,0,2,1:T(8,128)} fusion(f32[]{:T(128)} %bitcast.55, f32[]{:T(128)} %bitcast.54, f32[]{:T(128)} %bitcast.53, f32[]{:T(128)} %bitcast.52, f32[]{:T(128)} %bitcast.51, f32[]{:T(128)} %bitcast.50, f32[]{:T(128)} %bitcast.49, f32[]{:T(128)} %bitcast.48, f32[]{:T(128)} %bitcast.47, f32[]{:T(128)} %bitcast.46, ...), kind=kLoop, calls=%fused_computation.117 | loop fusion | flops 3276800 | bytes 4850216 | tf_op jit(solution)/shard_map/mul | solution.py:93
  181.9 8.2 %maximum_multiply_fusion.14 = f32[10,128,1,128]{3,0,2,1:T(8,128)} fusion(f32[]{:T(128)} %bitcast.36, f32[]{:T(128)} %bitcast.35, f32[]{:T(128)} %bitcast.34, f32[]{:T(128)} %bitcast.33, f32[]{:T(128)} %bitcast.32, f32[]{:T(128)} %bitcast.31, f32[]{:T(128)} %bitcast.30, f32[]{:T(128)} %bitcast.29, f32[]{:T(128)} %bitcast.28, f32[]{:T(128)} %bitcast.27, ...), kind=kLoop, calls=%fused_computation.118 | loop fusion | flops 3276800 | bytes 4850216 | tf_op jit(solution)/shard_map/mul | solution.py:93
  190.1 133.2 %fusion.610 = bf16[8,128,1,128]{3,0,2,1:T(8,128)(2,1)} fusion(f32[10,128,1,128]{3,0,2,1:T(8,128)S(1)} %maximum_multiply_fusion, f32[]{:T(128)} %bitcast.310, f32[]{:T(128)} %bitcast.309, f32[]{:T(128)} %bitcast.308, f32[]{:T(128)} %bitcast.307, f32[]{:T(128)} %bitcast.306, f32[]{:T(128)} %bitcast.305, f32[]{:T(128)} %bitcast.304, f32[]{:T(128)} %bitcast.303, ...), kind=kLoop, calls=%fused_computation.882 | loop fusion | flops 37486592 | bytes 42277376 | tf_op jit(solution)/shard_map/convert_element_type | solution.py:98
  381.7 7.3 %fusion.566 = f32[8,2,64,128]{3,0,1,2:T(8,128)S(1)} fusion(bf16[8,64,2,1,128]{4,0,2,1,3:T(8,128)(2,1)S(1)} %bitcast.888, f32[]{:T(128)} %bitcast.497, f32[]{:T(128)} %bitcast.496, f32[]{:T(128)} %bitcast.495, f32[]{:T(128)} %bitcast.494, f32[]{:T(128)} %bitcast.493, f32[]{:T(128)} %bitcast.492, f32[]{:T(128)} %bitcast.491, f32[]{:T(128)} %bitcast.490, ...), kind=kLoop, calls=%fused_computation.837 | loop fusion | flops 2621440 | bytes 1851432 | tf_op jit(solution)/shard_map/max | solution.py:42
  417.6 7.2 %fusion.531 = f32[8,2,64,128]{3,0,1,2:T(8,128)S(1)} fusion(bf16[8,64,2,1,128]{4,0,2,1,3:T(8,128)(2,1)S(1)} %bitcast.893, f32[]{:T(128)} %bitcast.402, f32[]{:T(128)} %bitcast.401, f32[]{:T(128)} %bitcast.400, f32[]{:T(128)} %bitcast.399, f32[]{:T(128)} %bitcast.398, f32[]{:T(128)} %bitcast.397, f32[]{:T(128)} %bitcast.396, f32[]{:T(128)} %bitcast.395, ...), kind=kLoop, calls=%fused_computation.802 | loop fusion | flops 2621440 | bytes 1851432 | tf_op jit(solution)/shard_map/max | solution.py:42
  424.9 7.2 %fusion.524 = f32[8,2,64,128]{3,0,1,2:T(8,128)S(1)} fusion(bf16[8,64,2,1,128]{4,0,2,1,3:T(8,128)(2,1)S(1)} %bitcast.894, f32[]{:T(128)} %bitcast.383, f32[]{:T(128)} %bitcast.382, f32[]{:T(128)} %bitcast.381, f32[]{:T(128)} %bitcast.380, f32[]{:T(128)} %bitcast.379, f32[]{:T(128)} %bitcast.378, f32[]{:T(128)} %bitcast.377, f32[]{:T(128)} %bitcast.376, ...), kind=kLoop, calls=%fused_computation.795 | loop fusion | flops 2621440 | bytes 1851432 | tf_op jit(solution)/shard_map/max | solution.py:42
  439.2 7.3 %fusion.510 = f32[8,2,64,128]{3,0,1,2:T(8,128)S(1)} fusion(bf16[8,64,2,1,128]{4,0,2,1,3:T(8,128)(2,1)S(1)} %bitcast.896, f32[]{:T(128)} %bitcast.345, f32[]{:T(128)} %bitcast.344, f32[]{:T(128)} %bitcast.343, f32[]{:T(128)} %bitcast.342, f32[]{:T(128)} %bitcast.341, f32[]{:T(128)} %bitcast.339, f32[]{:T(128)} %bitcast.338, f32[]{:T(128)} %bitcast.337, ...), kind=kLoop, calls=%fused_computation.781 | loop fusion | flops 2621440 | bytes 1851432 | tf_op jit(solution)/shard_map/max | solution.py:42
  446.6 7.9 %broadcast_multiply_fusion = (f32[8,2,64,128]{3,0,1,2:T(8,128)S(1)}, f32[8,2,64,128]{3,0,1,2:T(8,128)S(1)}) fusion(f32[]{:T(128)} %bitcast.329, f32[]{:T(128)} %bitcast.325, f32[]{:T(128)} %bitcast.324, f32[]{:T(128)} %bitcast.323, f32[]{:T(128)} %bitcast.322, f32[]{:T(128)} %bitcast.321, bf16[8,64,2,1,128]{4,0,2,1,3:T(8,128)(2,1)S(1)} %bitcast.897, ...), kind=kLoop, calls=%fused_computation.884 | loop fusion | flops 2752512 | bytes 2375724 | tf_op jit(solution)/shard_map/mul | solution.py:27
  454.6 105.9 %fusion.609 = bf16[8,2,64,128]{3,0,1,2:T(8,128)(2,1)S(1)} fusion(f32[8,2,66,128]{3,0,1,2:T(8,128)S(1)} %pad.206, f32[8,2,64,128]{3,0,1,2:T(8,128)S(1)} %fusion.608, f32[]{:T(128)} %bitcast.619, f32[]{:T(128)} %bitcast.618, f32[]{:T(128)} %bitcast.617, f32[]{:T(128)} %bitcast.616, f32[]{:T(128)} %bitcast.615, f32[]{:T(128)} %bitcast.614, f32[]{:T(128)} %bitcast.613, ...), kind=kLoop, calls=%fused_computation.881 | loop fusion | flops 37748736 | bytes 34079292 | tf_op jit(solution)/shard_map/convert_element_type | solution.py:107
  (98 shorter events, 145.7 us)
Async XLA Ops:
  0.0 49.5 %copy-start = (bf16[1,128,1024]{2,1,0:T(8,128)(2,1)S(1)}, bf16[1,128,1024]{2,1,0:T(8,128)(2,1)}, u32[]{:S(2)}) copy-start(bf16[1,128,1024]{2,1,0:T(8,128)(2,1)} %param.8) | copy-start | bytes 786436
  4.2 10.5 %copy-start.3 = (f32[16,9]{1,0:T(8,128)S(1)}, f32[16,9]{1,0:T(8,128)}, u32[]{:S(2)}) copy-start(f32[16,9]{1,0:T(8,128)} %param.10) | copy-start | bytes 1732
  4.2 11.2 %copy-start.2 = (f32[16,9]{1,0:T(8,128)S(1)}, f32[16,9]{1,0:T(8,128)}, u32[]{:S(2)}) copy-start(f32[16,9]{1,0:T(8,128)} %param.12) | copy-start | bytes 1732
  4.2 11.9 %copy-start.5 = (f32[16,9]{1,0:T(8,128)S(1)}, f32[16,9]{1,0:T(8,128)}, u32[]{:S(2)}) copy-start(f32[16,9]{1,0:T(8,128)} %param.13) | copy-start | bytes 1732
  4.2 12.7 %copy-start.6 = (f32[16]{0:T(128)S(1)}, f32[16]{0:T(128)}, u32[]{:S(2)}) copy-start(f32[16]{0:T(128)} %param.11) | copy-start | bytes 196
  4.2 13.4 %copy-start.7 = (f32[16]{0:T(128)S(1)}, f32[16]{0:T(128)}, u32[]{:S(2)}) copy-start(f32[16]{0:T(128)} %param.14) | copy-start | bytes 196
  4.2 16.3 %copy-start.4 = (f32[16,9]{1,0:T(8,128)S(1)}, f32[16,9]{1,0:T(8,128)}, u32[]{:S(2)}) copy-start(f32[16,9]{1,0:T(8,128)} %param.15) | copy-start | bytes 1732
  4.2 39.5 %all-to-all-start = ((bf16[64,8,2,1024]{3,2,1,0:T(2,128)(2,1)}), bf16[64,8,2,1024]{3,2,1,0:T(2,128)(2,1)S(1)}, u32[]{:S(2)}, u32[]{:S(2)}) async-start(bf16[64,8,2,1024]{3,2,1,0:T(2,128)(2,1)} %stack.2), calls=%async_computation | async-start | bytes 4194304 | tf_op jit(solution)/shard_map/all_to_all | solution.py:66
  50.3 8.8 %collective-permute-start.1 = (bf16[2,128,1,128]{3,0,2,1:T(2,128)(2,1)S(1)}, bf16[2,128,1,128]{3,0,2,1:T(2,128)(2,1)S(1)}, u32[]{:S(2)}, u32[]{:S(2)}) collective-permute-start(bf16[2,128,1,128]{3,0,2,1:T(2,128)(2,1)S(1)} %copy.15), channel_id=1, source_target_pairs={{1,0},{2,1},{3,2},{5,4},{6,5},{7,6},{9,8},{10,9},{11,10},{13,12},{... | collective-permute-start | bytes 196616 | tf_op jit(solution)/shard_map/ppermute | solution.py:15
  51.7 7.4 %collective-permute-start = (bf16[2,128,1,128]{3,0,2,1:T(2,128)(2,1)S(1)}, bf16[2,128,1,128]{3,0,2,1:T(2,128)(2,1)S(1)}, u32[]{:S(2)}, u32[]{:S(2)}) collective-permute-start(bf16[2,128,1,128]{3,0,2,1:T(2,128)(2,1)S(1)} %copy.14), channel_id=1, source_target_pairs={{0,1},{1,2},{2,3},{4,5},{5,6},{6,7},{8,9},{9,10},{10,11},{12,13},{... | collective-permute-start | bytes 196616 | tf_op jit(solution)/shard_map/ppermute | solution.py:12
  66.5 3.1 copy-start.1
  323.2 15.6 %all-to-all-start.1 = ((bf16[8,128,1,128]{3,0,2,1:T(8,128)(2,1)}), bf16[8,128,1,128]{3,0,2,1:T(8,128)(2,1)S(1)}, u32[]{:S(2)}, u32[]{:S(2)}) async-start(bf16[8,128,1,128]{3,0,2,1:T(8,128)(2,1)} %fusion.610), calls=%async_computation.1 | async-start | bytes 524288 | tf_op jit(solution)/shard_map/all_to_all | solution.py:100
